TPU v7x, 512 devices: a whole 4x8x8 slice. The times are simulated.
512 devices in a mesh: outer: 128 (over z, y, core), inner: 4 (over x).
Axes of the slice: x: 4, y: 8, z: 8, core: 2. Of those that a mesh axis runs over, the one named last changes fastest.
Arguments:
- query_states: bfloat16 [65536, 4096], P(('outer', 'inner')), may hold values from -6 to 6
- key_states: bfloat16 [65536, 4096], P(('outer', 'inner')), may hold values from -6 to 6
- value_states: bfloat16 [65536, 4096], P(('outer', 'inner')), may hold values from -6 to 6
- doc_lengths: int32 [128], replicated, may hold values from 1 to 1024, 65536 in all
- slopes: float32 [32], replicated, may hold values from 0.00024414062 to 0.0625
Outputs:
- attended: bfloat16 [65536, 4096], P(('outer', 'inner'))
Inputs may be any that keep to these rules, and one draw needn't show every extreme that they name: `doc_lengths`: the lengths add up to 65536; the longest is exactly 1024.
All inputs are finite; a program needn't handle non-finite values.
Results may differ from a plain program's by a relative error of at most 0.0045.
Values may be sent and summed in bfloat16 or wider, within the bound.
No kernel may reach another device: no remote copies, remote signals or barrier semaphores. Data moves between devices by JAX's collectives and lax.ppermute only.
A program may use at most 64 MiB of HBM per device.

v0:
```python
import math
import jax
import jax.numpy as jnp
from jax import lax
from jax.sharding import PartitionSpec as P

SPAN = 2
NEG_FILL = -1e30


def shifted(value, axis, steps):
    count = lax.axis_size(axis)
    first, last = (max(0, -steps), min(count, count - steps))
    return lax.ppermute(value, axis, [(source, source + steps) for source in range(first, last)])


def document_of(positions, doc_lengths):
    boundary = jnp.cumsum(doc_lengths)
    return jnp.sum((boundary[None, :] <= positions[:, None]).astype(jnp.int32), axis=1)


def empty_status(row_count, head_count, head_width):
    return (
        jnp.full((row_count, head_count), NEG_FILL, jnp.float32),
        jnp.zeros((row_count, head_count), jnp.float32),
        jnp.zeros((row_count, head_count, head_width), jnp.float32),
    )


def attend_block(status, query_parts, key_slab, value_slab, key_pos, key_doc, slopes):
    query_rows, query_pos, query_doc = query_parts
    allowed = (query_doc[:, None] == key_doc[None, :]) & (key_pos[None, :] <= query_pos[:, None])

    def update(current):
        running_max, row_total, weighted_sum = current
        scores = jnp.einsum(
            "qhd,khd->qhk", query_rows, key_slab, preferred_element_type=jnp.float32
        )
        scores = scores * (1.0 / math.sqrt(query_rows.shape[-1]))
        distance = (query_pos[:, None] - key_pos[None, :]).astype(jnp.float32)
        scores = scores - slopes[None, :, None] * distance[:, None, :]
        scores = jnp.where(allowed[:, None, :], scores, NEG_FILL)
        new_max = jnp.maximum(running_max, jnp.max(scores, axis=-1))
        weights = jnp.where(allowed[:, None, :], jnp.exp(scores - new_max[:, :, None]), 0.0)
        rescale = jnp.exp(running_max - new_max)
        row_total = row_total * rescale + jnp.sum(weights, axis=-1)
        products = jnp.einsum(
            "qhk,khd->qhd",
            weights.astype(jnp.bfloat16),
            value_slab,
            preferred_element_type=jnp.float32,
        )
        weighted_sum = weighted_sum * rescale[:, :, None] + products
        return (new_max, row_total, weighted_sum)

    def unchanged(current):
        return current

    return lax.cond(jnp.any(allowed), update, unchanged, status)


def attend_keys(status, query_parts, key_slab, value_slab, key_pos, slopes, doc_lengths):
    key_doc = document_of(key_pos, doc_lengths)
    key_count = key_slab.shape[0]
    slab_rows = 256
    pieces = key_count // slab_rows
    stacked = (
        key_slab.reshape((pieces, slab_rows) + key_slab.shape[1:]),
        value_slab.reshape((pieces, slab_rows) + value_slab.shape[1:]),
        key_pos.reshape(pieces, slab_rows),
        key_doc.reshape(pieces, slab_rows),
    )

    def scan_step(current, portion):
        return (
            attend_block(
                current, query_parts, portion[0], portion[1], portion[2], portion[3], slopes
            ),
            None,
        )

    result, unused = lax.scan(scan_step, status, stacked)
    return result


def combine(first_status, second_status):
    new_max = jnp.maximum(first_status[0], second_status[0])
    left_scale = jnp.exp(first_status[0] - new_max)
    right_scale = jnp.exp(second_status[0] - new_max)
    return (
        new_max,
        first_status[1] * left_scale + second_status[1] * right_scale,
        first_status[2] * left_scale[:, :, None] + second_status[2] * right_scale[:, :, None],
    )


def queries_from_later(query_rows, hops_back):
    return shifted(query_rows, "outer", -hops_back)


def partials_home(status, hops_back):
    running_max, row_total, weighted_sum = status
    moved_max, moved_total, moved_sum = shifted(
        (running_max, row_total, weighted_sum), "outer", hops_back
    )
    return (jnp.where(moved_total > 0.0, moved_max, NEG_FILL), moved_total, moved_sum)


def rows_of(status, slot_index, row_count):
    return tuple(
        (member[slot_index * row_count : (slot_index + 1) * row_count] for member in status)
    )


def bring_home(status, row_count, span_count):
    own_status = rows_of(status, 0, row_count)
    distant = [rows_of(status, hops_back, row_count) for hops_back in range(1, span_count + 1)]
    merged = own_status
    for hops_back in range(1, span_count + 1):
        merged = combine(merged, partials_home(distant[hops_back - 1], hops_back))
    return merged


def with_later_queries(own_rows, own_pos, group_rows, span_count, doc_lengths):
    rows_list = [own_rows]
    pos_list = [own_pos]
    for hops_back in range(1, span_count + 1):
        rows_list.append(queries_from_later(own_rows, hops_back))
        pos_list.append(own_pos + hops_back * group_rows)
    all_pos = jnp.concatenate(pos_list)
    return (jnp.concatenate(rows_list, axis=0), all_pos, document_of(all_pos, doc_lengths))


def normalize(status):
    return (status[2] / status[1][:, :, None]).astype(jnp.bfloat16)


def per_device(query_states, key_states, value_states, doc_lengths, slopes):
    rows_dev = query_states.shape[0]
    head_count = slopes.shape[0]
    head_width = query_states.shape[1] // head_count
    inner_count = lax.axis_size("inner")
    group_index = lax.axis_index("outer")
    inner_index = lax.axis_index("inner")
    group_rows = rows_dev * inner_count
    group_start = group_index * group_rows
    own_queries = query_states.reshape(rows_dev, head_count, head_width)
    own_pos = group_start + inner_index * rows_dev + jnp.arange(rows_dev, dtype=jnp.int32)
    query_parts = with_later_queries(own_queries, own_pos, group_rows, SPAN, doc_lengths)
    status = empty_status(query_parts[0].shape[0], head_count, head_width)
    portions = (
        lax.all_gather(
            key_states.reshape(rows_dev, head_count, head_width), "inner", axis=0, tiled=True
        ),
        lax.all_gather(
            value_states.reshape(rows_dev, head_count, head_width), "inner", axis=0, tiled=True
        ),
    )
    key_pos = group_start + jnp.arange(portions[0].shape[0], dtype=jnp.int32)
    status = attend_keys(
        status, query_parts, portions[0], portions[1], key_pos, slopes, doc_lengths
    )
    combined = bring_home(status, rows_dev, SPAN)
    return normalize(combined).reshape(rows_dev, head_count * head_width)


def solution(mesh):
    placed = (
        P(("outer", "inner"), None),
        P(("outer", "inner"), None),
        P(("outer", "inner"), None),
        P(),
        P(),
    )
    return jax.shard_map(
        per_device,
        mesh=mesh,
        in_specs=placed,
        out_specs=P(("outer", "inner"), None),
        check_vma=False,
    )
```

profile of v0, /device:TPU:256, one launch (start us, length us, event | category | flops | bytes accessed | tf_op | source)
XLA Modules:
  0.0 273.0 jit_solution(12478321590578903642)
XLA Ops:
  6.5 2.5 copy.32
  9.1 2.4 copy.33
  12.3 3.9 %collective-permute-start = (bf16[128,32,128]{0,2,1:T(8,128)(2,1)S(1)}, bf16[128,32,128]{0,2,1:T(8,128)(2,1)S(1)}, u32[]{:S(2)}, u32[]{:S(2)}) collective-permute-start(bf16[128,32,128]{0,2,1:T(8,128)(2,1)S(1)} %bitcast.49), channel_id=1, source_target_pairs={{4,0},{8,4},{12,8},{16,12},{20,16},{24,20},{28,24},{32,28},{36,32}... | collective-permute-start | bytes 3145736 | tf_op jit(solution)/shard_map/ppermute | solution.py:14
  16.2 3.3 %collective-permute-start.1 = (bf16[128,32,128]{0,2,1:T(8,128)(2,1)S(1)}, bf16[128,32,128]{0,2,1:T(8,128)(2,1)}, u32[]{:S(2)}, u32[]{:S(2)}) collective-permute-start(bf16[128,32,128]{0,2,1:T(8,128)(2,1)S(1)} %bitcast.50), channel_id=1, source_target_pairs={{8,0},{12,4},{16,8},{20,12},{24,16},{28,20},{32,24},{36,28},{40,32... | collective-permute-start | bytes 3145736 | tf_op jit(solution)/shard_map/ppermute | solution.py:14
  20.4 17.2 %collective-permute-done = bf16[128,32,128]{0,2,1:T(8,128)(2,1)S(1)} collective-permute-done((bf16[128,32,128]{0,2,1:T(8,128)(2,1)S(1)}, bf16[128,32,128]{0,2,1:T(8,128)(2,1)S(1)}, u32[]{:S(2)}, u32[]{:S(2)}) %collective-permute-start) | collective-permute-done | bytes 1048608 | tf_op jit(solution)/shard_map/ppermute | solution.py:14
  38.7 12.4 %collective-permute-done.1 = bf16[128,32,128]{0,2,1:T(8,128)(2,1)} collective-permute-done((bf16[128,32,128]{0,2,1:T(8,128)(2,1)S(1)}, bf16[128,32,128]{0,2,1:T(8,128)(2,1)}, u32[]{:S(2)}, u32[]{:S(2)}) %collective-permute-start.1) | collective-permute-done | bytes 1048608 | tf_op jit(solution)/shard_map/ppermute | solution.py:14
  51.1 2.4 pad_maximum_fusion
  53.5 2.9 %copy.27 = bf16[384,32,128]{2,0,1:T(8,128)(2,1)} copy(bf16[384,32,128]{0,2,1:T(8,128)(2,1)S(1)} %pad_maximum_fusion) | data formatting | bytes 6291456 | tf_op jit(solution)/shard_map/while | solution.py:82
  56.4 8.4 %all-gather.3.cloned.1.call-done = bf16[512,32,128]{2,1,0:T(8,128)(2,1)} async-done(((bf16[128,32,128]{2,1,0:T(8,128)(2,1)}), bf16[512,32,128]{2,1,0:T(8,128)(2,1)}) %all-gather.3.cloned.1.call-update) | async-done | bytes 4194320 | tf_op jit(solution)/shard_map/all_gather | solution.py:152
  64.8 5.8 %copy.26 = bf16[2,256,32,128]{3,1,2,0:T(8,128)(2,1)} copy(bf16[2,256,32,128]{3,2,1,0:T(8,128)(2,1)} %bitcast.45) | data formatting | bytes 8388608 | tf_op jit(solution)/shard_map/while | solution.py:82
  70.7 50.3 %all-gather.5.cloned.1.call-done = bf16[512,32,128]{2,1,0:T(8,128)(2,1)} async-done(((bf16[128,32,128]{2,1,0:T(8,128)(2,1)}), bf16[512,32,128]{2,1,0:T(8,128)(2,1)}) %all-gather.5.cloned.1.call-update) | async-done | bytes 4194320 | tf_op jit(solution)/shard_map/all_gather | solution.py:155
  121.0 6.0 %copy.28 = bf16[2,256,32,128]{3,1,2,0:T(8,128)(2,1)} copy(bf16[2,256,32,128]{3,2,1,0:T(8,128)(2,1)} %bitcast.46) | data formatting | bytes 8388608 | tf_op jit(solution)/shard_map/while | solution.py:82
  127.0 3.4 %broadcast_in_dim.61 = f32[384,32,128]{2,0,1:T(8,128)} broadcast(f32[]{:T(128)} %constant.59.clone.1), dimensions={} | broadcast | bytes 6291460 | tf_op jit(solution)/shard_map/broadcast_in_dim | solution.py:26
  130.4 41.3 %while.14 = (s32[]{:T(128)}, f32[384,32]{0,1:T(8,128)S(1)}, f32[384,32]{0,1:T(8,128)S(1)}, f32[384,32,128]{2,0,1:T(8,128)}, s32[384]{0:T(512)S(1)}, /*index=5*/s...) while((s32[]{:T(128)}, f32[384,32]{0,1:T(8,128)S(1)}, ...), condition=%wide.region_9.10_spmd, body=%wide.region_3.9_spmd.sunk | while | flops 1674141696 | bytes 104477920 | solution.py:82
  131.9 19.2 %conditional.2 = ((f32[384,32]{0,1:T(8,128)S(1)}, f32[384,32]{0,1:T(8,128)S(1)}, f32[384,32,128]{2,0,1:T(8,128)})) conditional(s32[]{:T(128)} %convert_element_type.41, (f32[384,32]{0,1:T(8,128)S(1)}, f32[384,32]{0,1:T(8,128)S(1)}, f32[384,32,128]{2,0,1:T(8,128)}) %tuple.50, (pred[384,256]{0,1:T(8,128)(4,1)S(1)}, bf16[2,256,32,128]{3,1,2,0:T(8,128)(2,1)}, ...), branch_computations={%region_5.5_spmd, %region_6.8_spmd} | conditional | flops 1673748480 | bytes 104370152 | solution.py:59
  132.0 4.5 %fusion.3 = (f32[384,32]{0,1:T(8,128)S(1)}, f32[32,256,384]{2,1,0:T(8,128)S(1)}) fusion(f32[384,256]{0,1:T(8,128)S(1)} %subtract_convert_fusion, f32[32]{0:T(128)S(1)} %get-tuple-element.141, pred[384,256]{0,1:T(8,128)(4,1)S(1)} %get-tuple-element.137, bf16[384,32,128]{2,0,1:T(8,128)(2,1)S(1)} %get-tuple-element.140, ...), kind=kOutput, calls=%fused_computation.5 | convolution fusion | flops 821022720 | bytes 18367104 | tf_op jit(solution)/shard_map/while/body/eval_jaxpr/cond/branch_1_fun/qhd,khd->qhk/dot_general | solution.py:36
  136.6 4.3 %fusion.2 = f32[384,32]{0,1:T(8,128)S(1)} fusion(f32[32,256,384]{2,1,0:T(8,128)S(1)} %get-tuple-element.239, f32[384,32]{0,1:T(8,128)S(1)} %max.8, f32[384,256]{0,1:T(8,128)S(1)} %subtract_convert_fusion, f32[32]{0:T(128)S(1)} %get-tuple-element.141, pred[384,256]{0,1:T(8,128)(4,1)S(1)} %get-tuple-element.137), kind=kLoop, calls=%fused_computation.4 | loop fusion | flops 22007808 | bytes 13172864 | tf_op jit(solution)/shard_map/while/body/eval_jaxpr/cond/branch_1_fun/reduce_sum | solution.py:46
  140.9 7.5 %bitcast_add_fusion = f32[384,32,128]{2,0,1:T(8,128)S(1)} fusion(f32[384,32,128]{2,0,1:T(8,128)S(1)} %bitcast.44, f32[384,32]{0,1:T(8,128)S(1)} %get-tuple-element.230, f32[32,256,384]{2,1,0:T(8,128)S(1)} %get-tuple-element.239, f32[384,32]{0,1:T(8,128)S(1)} %max.8, f32[384,256]{0,1:T(8,128)S(1)} %subtract_convert_fusion, f32[32]{0:T(128)S(1)} %get-tuple-element.141, ...), kind=kOutput, calls=%fused_computation.6 | convolution fusion | flops 830472192 | bytes 27853440 | tf_op jit(solution)/shard_map/while/body/eval_jaxpr/cond/branch_1_fun/qhk,khd->qhd/dot_general | solution.py:47
  148.4 2.7 copy-done
  152.5 19.2 %conditional.2 = ((f32[384,32]{0,1:T(8,128)S(1)}, f32[384,32]{0,1:T(8,128)S(1)}, f32[384,32,128]{2,0,1:T(8,128)})) conditional(s32[]{:T(128)} %convert_element_type.41, (f32[384,32]{0,1:T(8,128)S(1)}, f32[384,32]{0,1:T(8,128)S(1)}, f32[384,32,128]{2,0,1:T(8,128)}) %tuple.50, (pred[384,256]{0,1:T(8,128)(4,1)S(1)}, bf16[2,256,32,128]{3,1,2,0:T(8,128)(2,1)}, ...), branch_computations={%region_5.5_spmd, %region_6.8_spmd} | conditional | flops 1673748480 | bytes 104370152 | solution.py:59
  152.7 4.5 %fusion.3 = (f32[384,32]{0,1:T(8,128)S(1)}, f32[32,256,384]{2,1,0:T(8,128)S(1)}) fusion(f32[384,256]{0,1:T(8,128)S(1)} %subtract_convert_fusion, f32[32]{0:T(128)S(1)} %get-tuple-element.141, pred[384,256]{0,1:T(8,128)(4,1)S(1)} %get-tuple-element.137, bf16[384,32,128]{2,0,1:T(8,128)(2,1)S(1)} %get-tuple-element.140, ...), kind=kOutput, calls=%fused_computation.5 | convolution fusion | flops 821022720 | bytes 18367104 | tf_op jit(solution)/shard_map/while/body/eval_jaxpr/cond/branch_1_fun/qhd,khd->qhk/dot_general | solution.py:36
  157.2 4.3 %fusion.2 = f32[384,32]{0,1:T(8,128)S(1)} fusion(f32[32,256,384]{2,1,0:T(8,128)S(1)} %get-tuple-element.239, f32[384,32]{0,1:T(8,128)S(1)} %max.8, f32[384,256]{0,1:T(8,128)S(1)} %subtract_convert_fusion, f32[32]{0:T(128)S(1)} %get-tuple-element.141, pred[384,256]{0,1:T(8,128)(4,1)S(1)} %get-tuple-element.137), kind=kLoop, calls=%fused_computation.4 | loop fusion | flops 22007808 | bytes 13172864 | tf_op jit(solution)/shard_map/while/body/eval_jaxpr/cond/branch_1_fun/reduce_sum | solution.py:46
  161.6 7.5 %bitcast_add_fusion = f32[384,32,128]{2,0,1:T(8,128)S(1)} fusion(f32[384,32,128]{2,0,1:T(8,128)S(1)} %bitcast.44, f32[384,32]{0,1:T(8,128)S(1)} %get-tuple-element.230, f32[32,256,384]{2,1,0:T(8,128)S(1)} %get-tuple-element.239, f32[384,32]{0,1:T(8,128)S(1)} %max.8, f32[384,256]{0,1:T(8,128)S(1)} %subtract_convert_fusion, f32[32]{0:T(128)S(1)} %get-tuple-element.141, ...), kind=kOutput, calls=%fused_computation.6 | convolution fusion | flops 830472192 | bytes 27853440 | tf_op jit(solution)/shard_map/while/body/eval_jaxpr/cond/branch_1_fun/qhk,khd->qhd/dot_general | solution.py:47
  169.1 2.7 copy-done
  171.7 2.5 fusion.25
  176.1 3.4 %collective-permute-start.7 = (f32[128,32,128]{2,0,1:T(8,128)S(1)}, f32[128,32,128]{2,0,1:T(8,128)S(1)}, u32[]{:S(2)}, u32[]{:S(2)}) collective-permute-start(f32[128,32,128]{2,0,1:T(8,128)S(1)} %get-tuple-element.243), channel_id=1, source_target_pairs={{0,8},{4,12},{8,16},{12,20},{16,24},{20,28},{24,32},{28,36},{32,40... | collective-permute-start | bytes 6291464 | tf_op jit(solution)/shard_map/ppermute | solution.py:14
  179.6 3.2 %collective-permute-start.2 = (f32[128,32]{0,1:T(8,128)S(1)}, f32[128,32]{0,1:T(8,128)S(1)}, u32[]{:S(2)}, u32[]{:S(2)}) collective-permute-start(f32[128,32]{0,1:T(8,128)S(1)} %get-tuple-element.246), channel_id=1, source_target_pairs={{0,4},{4,8},{8,12},{12,16},{16,20},{20,24},{24,28},{28,32},{32,36}... | collective-permute-start | bytes 49160 | tf_op jit(solution)/shard_map/ppermute | solution.py:14
  182.8 2.2 collective-permute-start.3
  185.0 3.4 %collective-permute-start.5 = (f32[128,32]{0,1:T(8,128)S(1)}, f32[128,32]{0,1:T(8,128)S(1)}, u32[]{:S(2)}, u32[]{:S(2)}) collective-permute-start(f32[128,32]{0,1:T(8,128)S(1)} %get-tuple-element.247), channel_id=1, source_target_pairs={{0,8},{4,12},{8,16},{12,20},{16,24},{20,28},{24,32},{28,36},{32,40... | collective-permute-start | bytes 49160 | tf_op jit(solution)/shard_map/ppermute | solution.py:14
  188.4 61.8 %collective-permute-done.2 = f32[128,32]{0,1:T(8,128)S(1)} collective-permute-done((f32[128,32]{0,1:T(8,128)S(1)}, f32[128,32]{0,1:T(8,128)S(1)}, u32[]{:S(2)}, u32[]{:S(2)}) %collective-permute-start.2) | collective-permute-done | bytes 16416 | tf_op jit(solution)/shard_map/ppermute | solution.py:14
  252.1 7.0 %collective-permute-done.6 = f32[128,32]{0,1:T(8,128)S(1)} collective-permute-done((f32[128,32]{0,1:T(8,128)S(1)}, f32[128,32]{0,1:T(8,128)S(1)}, u32[]{:S(2)}, u32[]{:S(2)}) %collective-permute-start.6) | collective-permute-done | bytes 16416 | tf_op jit(solution)/shard_map/ppermute | solution.py:14
  259.2 7.0 %copy_bitcast_fusion = bf16[128,4096]{1,0:T(8,128)(2,1)} fusion(f32[128,32]{0,1:T(8,128)S(1)} %get-tuple-element.233, f32[128,32,128]{2,0,1:T(8,128)S(1)} %collective-permute-done.7, f32[128,32]{0,1:T(8,128)S(1)} %get-tuple-element.237, f32[128,32]{0,1:T(8,128)S(1)} %get-tuple-element.236, f32[128,32,128]{2,0,1:T(8,128)S(1)} %collective-permute-done.4, ...), kind=kLoop, calls=%fused_computation.27 | loop fusion | flops 4194304 | bytes 7421952 | tf_op jit(solution)/shard_map/reshape | solution.py:164
  (63 shorter events, 8.5 us)
Async XLA Ops:
  6.5 5.1 %copy-start.3 = (bf16[128,4096]{1,0:T(8,128)(2,1)S(1)}, bf16[128,4096]{1,0:T(8,128)(2,1)}, u32[]{:S(2)}) copy-start(bf16[128,4096]{1,0:T(8,128)(2,1)} %param.9) | copy-start | bytes 3145732
  6.5 12.9 %copy-start.6 = (s32[128]{0:T(128)S(1)}, s32[128]{0:T(128)}, u32[]{:S(2)}) copy-start(s32[128]{0:T(128)} %param.12) | copy-start | bytes 1540
  6.5 58.3 %all-gather.3.cloned.1.call-start = ((), (), s32[]{:S(2)}) async-start(), calls=%async_computation | async-start | bytes 5242880 | tf_op jit(solution)/shard_map/all_gather | solution.py:152
  9.1 111.9 %all-gather.5.cloned.1.call-start = ((), (), s32[]{:S(2)}) async-start(), calls=%async_computation.1 | async-start | bytes 5242880 | tf_op jit(solution)/shard_map/all_gather | solution.py:155
  12.3 25.4 %copy-start.1 = (bf16[128,4096]{0,1:T(8,128)(2,1)}, bf16[128,4096]{0,1:T(8,128)(2,1)S(1)}, u32[]{:S(2)}) copy-start(bf16[128,4096]{0,1:T(8,128)(2,1)S(1)} %copy.25) | copy-start | bytes 3145732
  12.3 25.4 %collective-permute-start = (bf16[128,32,128]{0,2,1:T(8,128)(2,1)S(1)}, bf16[128,32,128]{0,2,1:T(8,128)(2,1)S(1)}, u32[]{:S(2)}, u32[]{:S(2)}) collective-permute-start(bf16[128,32,128]{0,2,1:T(8,128)(2,1)S(1)} %bitcast.49), channel_id=1, source_target_pairs={{4,0},{8,4},{12,8},{16,12},{20,16},{24,20},{28,24},{32,28},{36,32}... | collective-permute-start | bytes 3145736 | tf_op jit(solution)/shard_map/ppermute | solution.py:14
  16.2 34.9 %collective-permute-start.1 = (bf16[128,32,128]{0,2,1:T(8,128)(2,1)S(1)}, bf16[128,32,128]{0,2,1:T(8,128)(2,1)}, u32[]{:S(2)}, u32[]{:S(2)}) collective-permute-start(bf16[128,32,128]{0,2,1:T(8,128)(2,1)S(1)} %bitcast.50), channel_id=1, source_target_pairs={{8,0},{12,4},{16,8},{20,12},{24,16},{28,20},{32,24},{36,28},{40,32... | collective-permute-start | bytes 3145736 | tf_op jit(solution)/shard_map/ppermute | solution.py:14
  37.6 1.0 copy-start.4
  121.0 9.4 %copy-start.2 = (bf16[384,32,128]{2,0,1:T(8,128)(2,1)S(1)}, bf16[384,32,128]{2,0,1:T(8,128)(2,1)}, u32[]{:S(2)}) copy-start(bf16[384,32,128]{2,0,1:T(8,128)(2,1)} %copy.27) | copy-start | bytes 9437188
  121.0 9.4 %copy-start.5 = (f32[32]{0:T(128)S(1)}, f32[32]{0:T(128)}, u32[]{:S(2)}) copy-start(f32[32]{0:T(128)} %param.13) | copy-start | bytes 388
  131.9 9.0 %slice-start = ((s8[6291456]{0:T(1024)(128)(4,1)}), s8[4194304]{0:T(1024)(128)(4,1)S(1)}, s32[]{:S(2)}) async-start(s8[6291456]{0:T(1024)(128)(4,1)} %bitcast.43), calls=%async_computation.2 | async-start | bytes 8388608 | tf_op jit(solution)/shard_map/while/body/eval_jaxpr/cond
  132.0 8.9 %slice-start.1 = ((s8[6291456]{0:T(1024)(128)(4,1)}), s8[2097152]{0:T(1024)(128)(4,1)S(1)}, s32[]{:S(2)}) async-start(s8[6291456]{0:T(1024)(128)(4,1)} %bitcast.43), calls=%async_computation.3 | async-start | bytes 4194304 | tf_op jit(solution)/shard_map/while/body/eval_jaxpr/cond
  148.4 2.7 copy-start
  152.5 9.0 %slice-start = ((s8[6291456]{0:T(1024)(128)(4,1)}), s8[4194304]{0:T(1024)(128)(4,1)S(1)}, s32[]{:S(2)}) async-start(s8[6291456]{0:T(1024)(128)(4,1)} %bitcast.43), calls=%async_computation.2 | async-start | bytes 8388608 | tf_op jit(solution)/shard_map/while/body/eval_jaxpr/cond
  152.7 8.9 %slice-start.1 = ((s8[6291456]{0:T(1024)(128)(4,1)}), s8[2097152]{0:T(1024)(128)(4,1)S(1)}, s32[]{:S(2)}) async-start(s8[6291456]{0:T(1024)(128)(4,1)} %bitcast.43), calls=%async_computation.3 | async-start | bytes 4194304 | tf_op jit(solution)/shard_map/while/body/eval_jaxpr/cond
  169.0 2.7 copy-start
  174.2 84.9 %collective-permute-start.4 = (f32[128,32,128]{2,0,1:T(8,128)S(1)}, f32[128,32,128]{2,0,1:T(8,128)S(1)}, u32[]{:S(2)}, u32[]{:S(2)}) collective-permute-start(f32[128,32,128]{2,0,1:T(8,128)S(1)} %get-tuple-element.242), channel_id=1, source_target_pairs={{0,4},{4,8},{8,12},{12,16},{16,20},{20,24},{24,28},{28,32},{32,36}... | collective-permute-start | bytes 6291464 | tf_op jit(solution)/shard_map/ppermute | solution.py:14
  176.1 83.0 %collective-permute-start.7 = (f32[128,32,128]{2,0,1:T(8,128)S(1)}, f32[128,32,128]{2,0,1:T(8,128)S(1)}, u32[]{:S(2)}, u32[]{:S(2)}) collective-permute-start(f32[128,32,128]{2,0,1:T(8,128)S(1)} %get-tuple-element.243), channel_id=1, source_target_pairs={{0,8},{4,12},{8,16},{12,20},{16,24},{20,28},{24,32},{28,36},{32,40... | collective-permute-start | bytes 6291464 | tf_op jit(solution)/shard_map/ppermute | solution.py:14
  179.6 70.6 %collective-permute-start.2 = (f32[128,32]{0,1:T(8,128)S(1)}, f32[128,32]{0,1:T(8,128)S(1)}, u32[]{:S(2)}, u32[]{:S(2)}) collective-permute-start(f32[128,32]{0,1:T(8,128)S(1)} %get-tuple-element.246), channel_id=1, source_target_pairs={{0,4},{4,8},{8,12},{12,16},{16,20},{20,24},{24,28},{28,32},{32,36}... | collective-permute-start | bytes 49160 | tf_op jit(solution)/shard_map/ppermute | solution.py:14
  182.8 69.3 %collective-permute-start.3 = (f32[128,32]{0,1:T(8,128)S(1)}, f32[128,32]{0,1:T(8,128)S(1)}, u32[]{:S(2)}, u32[]{:S(2)}) collective-permute-start(f32[128,32]{0,1:T(8,128)S(1)} %get-tuple-element.245), channel_id=1, source_target_pairs={{0,4},{4,8},{8,12},{12,16},{16,20},{20,24},{24,28},{28,32},{32,36}... | collective-permute-start | bytes 49160 | tf_op jit(solution)/shard_map/ppermute | solution.py:14
  185.0 67.1 %collective-permute-start.5 = (f32[128,32]{0,1:T(8,128)S(1)}, f32[128,32]{0,1:T(8,128)S(1)}, u32[]{:S(2)}, u32[]{:S(2)}) collective-permute-start(f32[128,32]{0,1:T(8,128)S(1)} %get-tuple-element.247), channel_id=1, source_target_pairs={{0,8},{4,12},{8,16},{12,20},{16,24},{20,28},{24,32},{28,36},{32,40... | collective-permute-start | bytes 49160 | tf_op jit(solution)/shard_map/ppermute | solution.py:14
  250.2 8.9 %collective-permute-start.6 = (f32[128,32]{0,1:T(8,128)S(1)}, f32[128,32]{0,1:T(8,128)S(1)}, u32[]{:S(2)}, u32[]{:S(2)}) collective-permute-start(f32[128,32]{0,1:T(8,128)S(1)} %get-tuple-element.244), channel_id=1, source_target_pairs={{0,8},{4,12},{8,16},{12,20},{16,24},{20,28},{24,32},{28,36},{32,40... | collective-permute-start | bytes 49160 | tf_op jit(solution)/shard_map/ppermute | solution.py:14
Sparse Core Ops, SparseCore 0:
  9.5 55.3 all-gather.2
  66.9 53.9 all-gather.4
where the time goes:
time: 274 us; the launch traced here: 273 us
  waiting for transfers between devices  157 us (57%)
  local copies, waits for them, and re-layouts  32.9 us (12%)
  matrix products  24 us (9%)
  starting transfers between devices  23.2 us (8%)
  other arithmetic  20.6 us (8%)
  between operations  13.6 us (5%)
    ppermute x8, waiting for transfers between devices, shifted(): lax.ppermute(value, axis, [(source, source + steps) for source in range(f...  98.4 us
    all_gather x1, waiting for transfers between devices, per_device(): lax.all_gather(value_states.reshape(rows_dev, head_count, head_width), 'i...  50.3 us
    ppermute x8, starting transfers between devices, shifted(): lax.ppermute(value, axis, [(source, source + steps) for source in range(f...  23.2 us
    dot_general x2, matrix products, update(): jnp.einsum('qhk,khd->qhd', weights.astype(jnp.bfloat16), value_slab, pref...  15 us
    while x3, local copies, waits for them, and re-layouts, attend_keys(): result, unused = lax.scan(scan_step, status, stacked)  14.8 us
    dot_general x2, matrix products, update(): jnp.einsum('qhd,khd->qhk', query_rows, key_slab, preferred_element_type=j...  9.01 us
    reduce_sum x2, other arithmetic, update(): row_total = row_total * rescale + jnp.sum(weights, axis=-1)  8.57 us
    all_gather x1, waiting for transfers between devices, per_device(): lax.all_gather(key_states.reshape(rows_dev, head_count, head_width), 'inn...  8.4 us
  transfers between devices with their start and end apart: 10, of which 6 were waited for; matrix products, arithmetic and copies ran while one was open for 6% of the time, Pallas kernels for 0%

commit v1 on v0

--- a/solution.py
+++ b/solution.py
@@ -6,6 +6,22 @@
 
 SPAN = 2
 NEG_FILL = -1e30
+
+
+def gather_around(x, axis, dim):
+    ways, here, step = (lax.axis_size(axis), lax.axis_index(axis), x.shape[dim])
+    shape = [n * ways if d == dim else n for d, n in enumerate(x.shape)]
+    full = lax.dynamic_update_slice_in_dim(jnp.zeros(shape, x.dtype), x, here * step, axis=dim)
+    going_up = going_down = x
+    for far in range(1, ways // 2 + 1):
+        going_up = lax.ppermute(going_up, axis, [(d, (d + 1) % ways) for d in range(ways)])
+        full = lax.dynamic_update_slice_in_dim(full, going_up, (here - far) % ways * step, axis=dim)
+        if 2 * far < ways:
+            going_down = lax.ppermute(going_down, axis, [(d, (d - 1) % ways) for d in range(ways)])
+            full = lax.dynamic_update_slice_in_dim(
+                full, going_down, (here + far) % ways * step, axis=dim
+            )
+    return full
 
 
 def shifted(value, axis, steps):
@@ -152,9 +168,7 @@
         lax.all_gather(
             key_states.reshape(rows_dev, head_count, head_width), "inner", axis=0, tiled=True
         ),
-        lax.all_gather(
-            value_states.reshape(rows_dev, head_count, head_width), "inner", axis=0, tiled=True
-        ),
+        gather_around(value_states.reshape(rows_dev, head_count, head_width), "inner", 0),
     )
     key_pos = group_start + jnp.arange(portions[0].shape[0], dtype=jnp.int32)
     status = attend_keys(

time: 274 us -> 255 us (0.931)
  waiting for transfers between devices: 157 us -> 116 us
  local copies, waits for them, and re-layouts: 32.9 us -> 45.7 us
  starting transfers between devices: 23.2 us -> 33.4 us
    all_gather x1 -> x0, waiting for transfers between devices: 50.3 us -> none  [per_device(): lax.all_gather(value_states.reshape(rows_dev, head_count, head_width), 'i...]
    ppermute x0 -> x3, waiting for transfers between devices: none -> 48.8 us  [the longest x2 43.4 us: gather_around(): lax.ppermute(going_up, axis, [(d, (d + 1) % ways) for d in range(ways)])]
    ppermute x8, waiting for transfers between devices: 98.4 us -> 66.8 us  [shifted(): lax.ppermute(value, axis, [(source, source + steps) for source in range(f...]
    ppermute x0 -> x3, starting transfers between devices: none -> 10.2 us  [the longest x2 6.51 us: gather_around(): lax.ppermute(going_up, axis, [(d, (d + 1) % ways) for d in range(ways)])]
    dynamic_update_slice x0 -> x4, local copies, waits for them, and re-layouts: none -> 9.18 us  [the longest x2 4.59 us: gather_around(): lax.dynamic_update_slice_in_dim(full, going_up, (here - far) % ways * ste...]
    all_gather x1, waiting for transfers between devices: 8.4 us -> 0.01 us  [per_device(): lax.all_gather(key_states.reshape(rows_dev, head_count, head_width), 'inn...]
    unnamed x15 -> x13, local copies, waits for them, and re-layouts: 6.67 us -> 7.52 us
  transfers between devices with their start and end apart: 10 -> 12, of which waited for: 6 -> 5; matrix products, arithmetic and copies ran while one was open for 6% -> 11% of each run, Pallas kernels for 0% -> 0%
where the time goes in v1:
time: 255 us; the launch traced here: 254 us
  waiting for transfers between devices  116 us (45%)
  local copies, waits for them, and re-layouts  45.7 us (18%)
  starting transfers between devices  33.4 us (13%)
  matrix products  24 us (9%)
  other arithmetic  20.6 us (8%)
  between operations  13.7 us (5%)
    ppermute x8, waiting for transfers between devices, shifted(): lax.ppermute(value, axis, [(source, source + steps) for source in range(f...  66.8 us
    ppermute x2, waiting for transfers between devices, gather_around(): lax.ppermute(going_up, axis, [(d, (d + 1) % ways) for d in range(ways)])  43.4 us
    ppermute x8, starting transfers between devices, shifted(): lax.ppermute(value, axis, [(source, source + steps) for source in range(f...  23.2 us
    dot_general x2, matrix products, update(): jnp.einsum('qhk,khd->qhd', weights.astype(jnp.bfloat16), value_slab, pref...  15 us
    while x3, local copies, waits for them, and re-layouts, attend_keys(): result, unused = lax.scan(scan_step, status, stacked)  14.9 us
    dot_general x2, matrix products, update(): jnp.einsum('qhd,khd->qhk', query_rows, key_slab, preferred_element_type=j...  9.02 us
    reduce_sum x2, other arithmetic, update(): row_total = row_total * rescale + jnp.sum(weights, axis=-1)  8.57 us
    unnamed x13, local copies, waits for them, and re-layouts  7.52 us
  transfers between devices with their start and end apart: 12, of which 5 were waited for; matrix products, arithmetic and copies ran while one was open for 11% of the time, Pallas kernels for 0%

profile of v1, /device:TPU:256, one launch (start us, length us, event | category | flops | bytes accessed | tf_op | source)
XLA Modules:
  0.0 254.5 jit_solution(5811066365782132320)
XLA Ops:
  9.0 2.5 copy.33
  11.5 3.4 %collective-permute-start.2 = (bf16[128,32,128]{2,1,0:T(8,128)(2,1)}, bf16[128,32,128]{2,1,0:T(8,128)(2,1)}, u32[]{:S(2)}, u32[]{:S(2)}) collective-permute-start(bf16[128,32,128]{2,1,0:T(8,128)(2,1)} %bitcast.15), channel_id=1, source_target_pairs={{0,1},{1,2},{2,3},{3,0},{4,5},{5,6},{6,7},{7,4},{8,9},{9,10},{10,1... | collective-permute-start | bytes 3145736 | tf_op jit(solution)/shard_map/ppermute | solution.py:17
  16.5 3.6 %collective-permute-start = (bf16[128,32,128]{0,2,1:T(8,128)(2,1)S(1)}, bf16[128,32,128]{0,2,1:T(8,128)(2,1)S(1)}, u32[]{:S(2)}, u32[]{:S(2)}) collective-permute-start(bf16[128,32,128]{0,2,1:T(8,128)(2,1)S(1)} %bitcast.47), channel_id=1, source_target_pairs={{4,0},{8,4},{12,8},{16,12},{20,16},{24,20},{28,24},{32,28},{36,32}... | collective-permute-start | bytes 3145736 | tf_op jit(solution)/shard_map/ppermute | solution.py:30
  20.1 3.3 %collective-permute-start.1 = (bf16[128,32,128]{0,2,1:T(8,128)(2,1)S(1)}, bf16[128,32,128]{0,2,1:T(8,128)(2,1)}, u32[]{:S(2)}, u32[]{:S(2)}) collective-permute-start(bf16[128,32,128]{0,2,1:T(8,128)(2,1)S(1)} %bitcast.48), channel_id=1, source_target_pairs={{8,0},{12,4},{16,8},{20,12},{24,16},{28,20},{32,24},{36,28},{40,32... | collective-permute-start | bytes 3145736 | tf_op jit(solution)/shard_map/ppermute | solution.py:30
  23.4 3.7 %collective-permute-start.3 = (bf16[128,32,128]{2,1,0:T(8,128)(2,1)}, bf16[128,32,128]{2,1,0:T(8,128)(2,1)}, u32[]{:S(2)}, u32[]{:S(2)}) collective-permute-start(bf16[128,32,128]{2,1,0:T(8,128)(2,1)} %bitcast.15), channel_id=1, source_target_pairs={{0,3},{1,0},{2,1},{3,2},{4,7},{5,4},{6,5},{7,6},{8,11},{9,8},{10,9... | collective-permute-start | bytes 3145736 | tf_op jit(solution)/shard_map/ppermute | solution.py:20
  27.8 21.9 %collective-permute-done.2 = bf16[128,32,128]{2,1,0:T(8,128)(2,1)} collective-permute-done((bf16[128,32,128]{2,1,0:T(8,128)(2,1)}, bf16[128,32,128]{2,1,0:T(8,128)(2,1)}, u32[]{:S(2)}, u32[]{:S(2)}) %collective-permute-start.2) | collective-permute-done | bytes 1048608 | tf_op jit(solution)/shard_map/ppermute | solution.py:17
  49.7 3.1 %collective-permute-start.4 = (bf16[128,32,128]{2,1,0:T(8,128)(2,1)}, bf16[128,32,128]{2,1,0:T(8,128)(2,1)}, u32[]{:S(2)}, u32[]{:S(2)}) collective-permute-start(bf16[128,32,128]{2,1,0:T(8,128)(2,1)} %collective-permute-done.2), channel_id=1, source_target_pairs={{0,1},{1,2},{2,3},{3,0},{4,5},{5,6},{6,7},{7,4},{8,9},{9,10},{10,1... | collective-permute-start | bytes 3145736 | tf_op jit(solution)/shard_map/ppermute | solution.py:17
  53.1 2.6 %broadcast_in_dim.65 = bf16[512,32,128]{2,1,0:T(8,128)(2,1)} broadcast(bf16[]{:T(256)} %constant.83.clone.1), dimensions={} | broadcast | bytes 4194306 | tf_op jit(solution)/shard_map/broadcast_in_dim | solution.py:14
  61.4 3.1 %copy.27 = bf16[384,32,128]{2,0,1:T(8,128)(2,1)} copy(bf16[384,32,128]{0,2,1:T(8,128)(2,1)S(1)} %pad_maximum_fusion) | data formatting | bytes 6291456 | tf_op jit(solution)/shard_map/while | solution.py:98
  66.7 5.4 %collective-permute-done.3 = bf16[128,32,128]{2,1,0:T(8,128)(2,1)} collective-permute-done((bf16[128,32,128]{2,1,0:T(8,128)(2,1)}, bf16[128,32,128]{2,1,0:T(8,128)(2,1)}, u32[]{:S(2)}, u32[]{:S(2)}) %collective-permute-start.3) | collective-permute-done | bytes 1048608 | tf_op jit(solution)/shard_map/ppermute | solution.py:20
  74.4 21.5 %collective-permute-done.4 = bf16[128,32,128]{2,1,0:T(8,128)(2,1)} collective-permute-done((bf16[128,32,128]{2,1,0:T(8,128)(2,1)}, bf16[128,32,128]{2,1,0:T(8,128)(2,1)}, u32[]{:S(2)}, u32[]{:S(2)}) %collective-permute-start.4) | collective-permute-done | bytes 1048608 | tf_op jit(solution)/shard_map/ppermute | solution.py:17
  98.3 5.8 %copy.28 = bf16[2,256,32,128]{3,1,2,0:T(8,128)(2,1)} copy(bf16[2,256,32,128]{3,2,1,0:T(8,128)(2,1)} %bitcast.9) | data formatting | bytes 8388608 | tf_op jit(solution)/shard_map/while | solution.py:98
  104.1 6.0 %copy.26 = bf16[2,256,32,128]{3,1,2,0:T(8,128)(2,1)} copy(bf16[2,256,32,128]{3,2,1,0:T(8,128)(2,1)} %bitcast.45) | data formatting | bytes 8388608 | tf_op jit(solution)/shard_map/while | solution.py:98
  110.1 3.4 %broadcast_in_dim.64 = f32[384,32,128]{2,0,1:T(8,128)} broadcast(f32[]{:T(128)} %constant.82.clone.1), dimensions={} | broadcast | bytes 6291460 | tf_op jit(solution)/shard_map/broadcast_in_dim | solution.py:42
  113.6 41.3 %while.14 = (s32[]{:T(128)}, f32[384,32]{0,1:T(8,128)S(1)}, f32[384,32]{0,1:T(8,128)S(1)}, f32[384,32,128]{2,0,1:T(8,128)}, s32[384]{0:T(512)S(1)}, /*index=5*/s...) while((s32[]{:T(128)}, f32[384,32]{0,1:T(8,128)S(1)}, ...), condition=%wide.region_9.10_spmd, body=%wide.region_3.9_spmd.sunk | while | flops 1674141696 | bytes 104477920 | solution.py:98
  115.1 19.2 %conditional.2 = ((f32[384,32]{0,1:T(8,128)S(1)}, f32[384,32]{0,1:T(8,128)S(1)}, f32[384,32,128]{2,0,1:T(8,128)})) conditional(s32[]{:T(128)} %convert_element_type.41, (f32[384,32]{0,1:T(8,128)S(1)}, f32[384,32]{0,1:T(8,128)S(1)}, f32[384,32,128]{2,0,1:T(8,128)}) %tuple.50, (pred[384,256]{0,1:T(8,128)(4,1)S(1)}, bf16[2,256,32,128]{3,1,2,0:T(8,128)(2,1)}, ...), branch_computations={%region_5.5_spmd, %region_6.8_spmd} | conditional | flops 1673748480 | bytes 104370152 | solution.py:75
  115.2 4.5 %fusion.3 = (f32[384,32]{0,1:T(8,128)S(1)}, f32[32,256,384]{2,1,0:T(8,128)S(1)}) fusion(f32[384,256]{0,1:T(8,128)S(1)} %subtract_convert_fusion, f32[32]{0:T(128)S(1)} %get-tuple-element.141, pred[384,256]{0,1:T(8,128)(4,1)S(1)} %get-tuple-element.137, bf16[384,32,128]{2,0,1:T(8,128)(2,1)S(1)} %get-tuple-element.140, ...), kind=kOutput, calls=%fused_computation.5 | convolution fusion | flops 821022720 | bytes 18367104 | tf_op jit(solution)/shard_map/while/body/eval_jaxpr/cond/branch_1_fun/qhd,khd->qhk/dot_general | solution.py:52
  119.7 4.3 %fusion.2 = f32[384,32]{0,1:T(8,128)S(1)} fusion(f32[32,256,384]{2,1,0:T(8,128)S(1)} %get-tuple-element.239, f32[384,32]{0,1:T(8,128)S(1)} %max.8, f32[384,256]{0,1:T(8,128)S(1)} %subtract_convert_fusion, f32[32]{0:T(128)S(1)} %get-tuple-element.141, pred[384,256]{0,1:T(8,128)(4,1)S(1)} %get-tuple-element.137), kind=kLoop, calls=%fused_computation.4 | loop fusion | flops 22007808 | bytes 13172864 | tf_op jit(solution)/shard_map/while/body/eval_jaxpr/cond/branch_1_fun/reduce_sum | solution.py:62
  124.1 7.5 %bitcast_add_fusion = f32[384,32,128]{2,0,1:T(8,128)S(1)} fusion(f32[384,32,128]{2,0,1:T(8,128)S(1)} %bitcast.44, f32[384,32]{0,1:T(8,128)S(1)} %get-tuple-element.230, f32[32,256,384]{2,1,0:T(8,128)S(1)} %get-tuple-element.239, f32[384,32]{0,1:T(8,128)S(1)} %max.8, f32[384,256]{0,1:T(8,128)S(1)} %subtract_convert_fusion, f32[32]{0:T(128)S(1)} %get-tuple-element.141, ...), kind=kOutput, calls=%fused_computation.6 | convolution fusion | flops 830472192 | bytes 27853440 | tf_op jit(solution)/shard_map/while/body/eval_jaxpr/cond/branch_1_fun/qhk,khd->qhd/dot_general | solution.py:63
  131.6 2.7 %copy-done = f32[384,32,128]{2,0,1:T(8,128)} copy-done((f32[384,32,128]{2,0,1:T(8,128)}, f32[384,32,128]{2,0,1:T(8,128)S(1)}, u32[]{:S(2)}) %copy-start) | copy-done | bytes 6291480 | tf_op jit(solution)/shard_map/while/body/eval_jaxpr/cond
  135.7 19.2 %conditional.2 = ((f32[384,32]{0,1:T(8,128)S(1)}, f32[384,32]{0,1:T(8,128)S(1)}, f32[384,32,128]{2,0,1:T(8,128)})) conditional(s32[]{:T(128)} %convert_element_type.41, (f32[384,32]{0,1:T(8,128)S(1)}, f32[384,32]{0,1:T(8,128)S(1)}, f32[384,32,128]{2,0,1:T(8,128)}) %tuple.50, (pred[384,256]{0,1:T(8,128)(4,1)S(1)}, bf16[2,256,32,128]{3,1,2,0:T(8,128)(2,1)}, ...), branch_computations={%region_5.5_spmd, %region_6.8_spmd} | conditional | flops 1673748480 | bytes 104370152 | solution.py:75
  135.9 4.5 %fusion.3 = (f32[384,32]{0,1:T(8,128)S(1)}, f32[32,256,384]{2,1,0:T(8,128)S(1)}) fusion(f32[384,256]{0,1:T(8,128)S(1)} %subtract_convert_fusion, f32[32]{0:T(128)S(1)} %get-tuple-element.141, pred[384,256]{0,1:T(8,128)(4,1)S(1)} %get-tuple-element.137, bf16[384,32,128]{2,0,1:T(8,128)(2,1)S(1)} %get-tuple-element.140, ...), kind=kOutput, calls=%fused_computation.5 | convolution fusion | flops 821022720 | bytes 18367104 | tf_op jit(solution)/shard_map/while/body/eval_jaxpr/cond/branch_1_fun/qhd,khd->qhk/dot_general | solution.py:52
  140.4 4.3 %fusion.2 = f32[384,32]{0,1:T(8,128)S(1)} fusion(f32[32,256,384]{2,1,0:T(8,128)S(1)} %get-tuple-element.239, f32[384,32]{0,1:T(8,128)S(1)} %max.8, f32[384,256]{0,1:T(8,128)S(1)} %subtract_convert_fusion, f32[32]{0:T(128)S(1)} %get-tuple-element.141, pred[384,256]{0,1:T(8,128)(4,1)S(1)} %get-tuple-element.137), kind=kLoop, calls=%fused_computation.4 | loop fusion | flops 22007808 | bytes 13172864 | tf_op jit(solution)/shard_map/while/body/eval_jaxpr/cond/branch_1_fun/reduce_sum | solution.py:62
  144.8 7.5 %bitcast_add_fusion = f32[384,32,128]{2,0,1:T(8,128)S(1)} fusion(f32[384,32,128]{2,0,1:T(8,128)S(1)} %bitcast.44, f32[384,32]{0,1:T(8,128)S(1)} %get-tuple-element.230, f32[32,256,384]{2,1,0:T(8,128)S(1)} %get-tuple-element.239, f32[384,32]{0,1:T(8,128)S(1)} %max.8, f32[384,256]{0,1:T(8,128)S(1)} %subtract_convert_fusion, f32[32]{0:T(128)S(1)} %get-tuple-element.141, ...), kind=kOutput, calls=%fused_computation.6 | convolution fusion | flops 830472192 | bytes 27853440 | tf_op jit(solution)/shard_map/while/body/eval_jaxpr/cond/branch_1_fun/qhk,khd->qhd/dot_general | solution.py:63
  152.3 2.7 %copy-done = f32[384,32,128]{2,0,1:T(8,128)} copy-done((f32[384,32,128]{2,0,1:T(8,128)}, f32[384,32,128]{2,0,1:T(8,128)S(1)}, u32[]{:S(2)}) %copy-start) | copy-done | bytes 6291480 | tf_op jit(solution)/shard_map/while/body/eval_jaxpr/cond
  154.9 2.5 fusion.25
  157.4 3.5 %collective-permute-start.10 = (f32[128,32,128]{2,0,1:T(8,128)S(1)}, f32[128,32,128]{2,0,1:T(8,128)S(1)}, u32[]{:S(2)}, u32[]{:S(2)}) collective-permute-start(f32[128,32,128]{2,0,1:T(8,128)S(1)} %get-tuple-element.243), channel_id=1, source_target_pairs={{0,8},{4,12},{8,16},{12,20},{16,24},{20,28},{24,32},{28,36},{32,40... | collective-permute-start | bytes 6291464 | tf_op jit(solution)/shard_map/ppermute | solution.py:30
  162.9 3.6 %collective-permute-start.5 = (f32[128,32]{0,1:T(8,128)S(1)}, f32[128,32]{0,1:T(8,128)S(1)}, u32[]{:S(2)}, u32[]{:S(2)}) collective-permute-start(f32[128,32]{0,1:T(8,128)S(1)} %get-tuple-element.246), channel_id=1, source_target_pairs={{0,4},{4,8},{8,12},{12,16},{16,20},{20,24},{24,28},{28,32},{32,36}... | collective-permute-start | bytes 49160 | tf_op jit(solution)/shard_map/ppermute | solution.py:30
  168.4 3.5 %collective-permute-start.8 = (f32[128,32]{0,1:T(8,128)S(1)}, f32[128,32]{0,1:T(8,128)S(1)}, u32[]{:S(2)}, u32[]{:S(2)}) collective-permute-start(f32[128,32]{0,1:T(8,128)S(1)} %get-tuple-element.247), channel_id=1, source_target_pairs={{0,8},{4,12},{8,16},{12,20},{16,24},{20,28},{24,32},{28,36},{32,40... | collective-permute-start | bytes 49160 | tf_op jit(solution)/shard_map/ppermute | solution.py:30
  171.9 59.8 %collective-permute-done.5 = f32[128,32]{0,1:T(8,128)S(1)} collective-permute-done((f32[128,32]{0,1:T(8,128)S(1)}, f32[128,32]{0,1:T(8,128)S(1)}, u32[]{:S(2)}, u32[]{:S(2)}) %collective-permute-start.5) | collective-permute-done | bytes 16416 | tf_op jit(solution)/shard_map/ppermute | solution.py:30
  233.6 7.0 %collective-permute-done.9 = f32[128,32]{0,1:T(8,128)S(1)} collective-permute-done((f32[128,32]{0,1:T(8,128)S(1)}, f32[128,32]{0,1:T(8,128)S(1)}, u32[]{:S(2)}, u32[]{:S(2)}) %collective-permute-start.9) | collective-permute-done | bytes 16416 | tf_op jit(solution)/shard_map/ppermute | solution.py:30
  240.7 7.0 %copy_bitcast_fusion = bf16[128,4096]{1,0:T(8,128)(2,1)} fusion(f32[128,32]{0,1:T(8,128)S(1)} %get-tuple-element.233, f32[128,32,128]{2,0,1:T(8,128)S(1)} %collective-permute-done.10, f32[128,32]{0,1:T(8,128)S(1)} %get-tuple-element.237, f32[128,32]{0,1:T(8,128)S(1)} %get-tuple-element.236, f32[128,32,128]{2,0,1:T(8,128)S(1)} %collective-permute-done.7, ...), kind=kLoop, calls=%fused_computation.27 | loop fusion | flops 4194304 | bytes 7421952 | tf_op jit(solution)/shard_map/reshape | solution.py:178
  (69 shorter events, 25.2 us)
Async XLA Ops:
  6.5 20.6 %copy-start.5 = (s32[128]{0:T(128)S(1)}, s32[128]{0:T(128)}, u32[]{:S(2)}) copy-start(s32[128]{0:T(128)} %param.12) | copy-start | bytes 1540
  6.5 97.6 %all-gather.2.cloned.1.call-start = ((), (), s32[]{:S(2)}) async-start(), calls=%async_computation | async-start | bytes 5242880 | tf_op jit(solution)/shard_map/all_gather | solution.py:168
  11.5 38.3 %collective-permute-start.2 = (bf16[128,32,128]{2,1,0:T(8,128)(2,1)}, bf16[128,32,128]{2,1,0:T(8,128)(2,1)}, u32[]{:S(2)}, u32[]{:S(2)}) collective-permute-start(bf16[128,32,128]{2,1,0:T(8,128)(2,1)} %bitcast.15), channel_id=1, source_target_pairs={{0,1},{1,2},{2,3},{3,0},{4,5},{5,6},{6,7},{7,4},{8,9},{9,10},{10,1... | collective-permute-start | bytes 3145736 | tf_op jit(solution)/shard_map/ppermute | solution.py:17
  16.5 41.5 %copy-start.1 = (bf16[128,4096]{0,1:T(8,128)(2,1)}, bf16[128,4096]{0,1:T(8,128)(2,1)S(1)}, u32[]{:S(2)}) copy-start(bf16[128,4096]{0,1:T(8,128)(2,1)S(1)} %copy.25) | copy-start | bytes 3145732
  16.5 41.5 %collective-permute-start = (bf16[128,32,128]{0,2,1:T(8,128)(2,1)S(1)}, bf16[128,32,128]{0,2,1:T(8,128)(2,1)S(1)}, u32[]{:S(2)}, u32[]{:S(2)}) collective-permute-start(bf16[128,32,128]{0,2,1:T(8,128)(2,1)S(1)} %bitcast.47), channel_id=1, source_target_pairs={{4,0},{8,4},{12,8},{16,12},{20,16},{24,20},{28,24},{32,28},{36,32}... | collective-permute-start | bytes 3145736 | tf_op jit(solution)/shard_map/ppermute | solution.py:30
  20.1 38.9 %collective-permute-start.1 = (bf16[128,32,128]{0,2,1:T(8,128)(2,1)S(1)}, bf16[128,32,128]{0,2,1:T(8,128)(2,1)}, u32[]{:S(2)}, u32[]{:S(2)}) collective-permute-start(bf16[128,32,128]{0,2,1:T(8,128)(2,1)S(1)} %bitcast.48), channel_id=1, source_target_pairs={{8,0},{12,4},{16,8},{20,12},{24,16},{28,20},{32,24},{36,28},{40,32... | collective-permute-start | bytes 3145736 | tf_op jit(solution)/shard_map/ppermute | solution.py:30
  23.4 48.7 %collective-permute-start.3 = (bf16[128,32,128]{2,1,0:T(8,128)(2,1)}, bf16[128,32,128]{2,1,0:T(8,128)(2,1)}, u32[]{:S(2)}, u32[]{:S(2)}) collective-permute-start(bf16[128,32,128]{2,1,0:T(8,128)(2,1)} %bitcast.15), channel_id=1, source_target_pairs={{0,3},{1,0},{2,1},{3,2},{4,7},{5,4},{6,5},{7,6},{8,11},{9,8},{10,9... | collective-permute-start | bytes 3145736 | tf_op jit(solution)/shard_map/ppermute | solution.py:20
  49.7 46.2 %collective-permute-start.4 = (bf16[128,32,128]{2,1,0:T(8,128)(2,1)}, bf16[128,32,128]{2,1,0:T(8,128)(2,1)}, u32[]{:S(2)}, u32[]{:S(2)}) collective-permute-start(bf16[128,32,128]{2,1,0:T(8,128)(2,1)} %collective-permute-done.2), channel_id=1, source_target_pairs={{0,1},{1,2},{2,3},{3,0},{4,5},{5,6},{6,7},{7,4},{8,9},{9,10},{10,1... | collective-permute-start | bytes 3145736 | tf_op jit(solution)/shard_map/ppermute | solution.py:17
  58.0 1.0 copy-start.3
  104.1 9.4 %copy-start.2 = (bf16[384,32,128]{2,0,1:T(8,128)(2,1)S(1)}, bf16[384,32,128]{2,0,1:T(8,128)(2,1)}, u32[]{:S(2)}) copy-start(bf16[384,32,128]{2,0,1:T(8,128)(2,1)} %copy.27) | copy-start | bytes 9437188
  104.1 9.4 %copy-start.4 = (f32[32]{0:T(128)S(1)}, f32[32]{0:T(128)}, u32[]{:S(2)}) copy-start(f32[32]{0:T(128)} %param.13) | copy-start | bytes 388
  115.1 9.0 %slice-start = ((s8[6291456]{0:T(1024)(128)(4,1)}), s8[4194304]{0:T(1024)(128)(4,1)S(1)}, s32[]{:S(2)}) async-start(s8[6291456]{0:T(1024)(128)(4,1)} %bitcast.43), calls=%async_computation.1 | async-start | bytes 8388608 | tf_op jit(solution)/shard_map/while/body/eval_jaxpr/cond
  115.2 8.9 %slice-start.1 = ((s8[6291456]{0:T(1024)(128)(4,1)}), s8[2097152]{0:T(1024)(128)(4,1)S(1)}, s32[]{:S(2)}) async-start(s8[6291456]{0:T(1024)(128)(4,1)} %bitcast.43), calls=%async_computation.2 | async-start | bytes 4194304 | tf_op jit(solution)/shard_map/while/body/eval_jaxpr/cond
  131.6 2.7 %copy-start = (f32[384,32,128]{2,0,1:T(8,128)}, f32[384,32,128]{2,0,1:T(8,128)S(1)}, u32[]{:S(2)}) copy-start(f32[384,32,128]{2,0,1:T(8,128)S(1)} %bitcast_add_fusion) | copy-start | bytes 18874372 | tf_op jit(solution)/shard_map/while/body/eval_jaxpr/cond
  135.7 9.0 %slice-start = ((s8[6291456]{0:T(1024)(128)(4,1)}), s8[4194304]{0:T(1024)(128)(4,1)S(1)}, s32[]{:S(2)}) async-start(s8[6291456]{0:T(1024)(128)(4,1)} %bitcast.43), calls=%async_computation.1 | async-start | bytes 8388608 | tf_op jit(solution)/shard_map/while/body/eval_jaxpr/cond
  135.8 8.9 %slice-start.1 = ((s8[6291456]{0:T(1024)(128)(4,1)}), s8[2097152]{0:T(1024)(128)(4,1)S(1)}, s32[]{:S(2)}) async-start(s8[6291456]{0:T(1024)(128)(4,1)} %bitcast.43), calls=%async_computation.2 | async-start | bytes 4194304 | tf_op jit(solution)/shard_map/while/body/eval_jaxpr/cond
  152.2 2.7 %copy-start = (f32[384,32,128]{2,0,1:T(8,128)}, f32[384,32,128]{2,0,1:T(8,128)S(1)}, u32[]{:S(2)}) copy-start(f32[384,32,128]{2,0,1:T(8,128)S(1)} %bitcast_add_fusion) | copy-start | bytes 18874372 | tf_op jit(solution)/shard_map/while/body/eval_jaxpr/cond
  157.4 83.2 %collective-permute-start.10 = (f32[128,32,128]{2,0,1:T(8,128)S(1)}, f32[128,32,128]{2,0,1:T(8,128)S(1)}, u32[]{:S(2)}, u32[]{:S(2)}) collective-permute-start(f32[128,32,128]{2,0,1:T(8,128)S(1)} %get-tuple-element.243), channel_id=1, source_target_pairs={{0,8},{4,12},{8,16},{12,20},{16,24},{20,28},{24,32},{28,36},{32,40... | collective-permute-start | bytes 6291464 | tf_op jit(solution)/shard_map/ppermute | solution.py:30
  160.9 79.7 %collective-permute-start.7 = (f32[128,32,128]{2,0,1:T(8,128)S(1)}, f32[128,32,128]{2,0,1:T(8,128)S(1)}, u32[]{:S(2)}, u32[]{:S(2)}) collective-permute-start(f32[128,32,128]{2,0,1:T(8,128)S(1)} %get-tuple-element.242), channel_id=1, source_target_pairs={{0,4},{4,8},{8,12},{12,16},{16,20},{20,24},{24,28},{28,32},{32,36}... | collective-permute-start | bytes 6291464 | tf_op jit(solution)/shard_map/ppermute | solution.py:30
  162.9 68.8 %collective-permute-start.5 = (f32[128,32]{0,1:T(8,128)S(1)}, f32[128,32]{0,1:T(8,128)S(1)}, u32[]{:S(2)}, u32[]{:S(2)}) collective-permute-start(f32[128,32]{0,1:T(8,128)S(1)} %get-tuple-element.246), channel_id=1, source_target_pairs={{0,4},{4,8},{8,12},{12,16},{16,20},{20,24},{24,28},{28,32},{32,36}... | collective-permute-start | bytes 49160 | tf_op jit(solution)/shard_map/ppermute | solution.py:30
  166.5 67.1 %collective-permute-start.6 = (f32[128,32]{0,1:T(8,128)S(1)}, f32[128,32]{0,1:T(8,128)S(1)}, u32[]{:S(2)}, u32[]{:S(2)}) collective-permute-start(f32[128,32]{0,1:T(8,128)S(1)} %get-tuple-element.245), channel_id=1, source_target_pairs={{0,4},{4,8},{8,12},{12,16},{16,20},{20,24},{24,28},{28,32},{32,36}... | collective-permute-start | bytes 49160 | tf_op jit(solution)/shard_map/ppermute | solution.py:30
  168.4 65.2 %collective-permute-start.8 = (f32[128,32]{0,1:T(8,128)S(1)}, f32[128,32]{0,1:T(8,128)S(1)}, u32[]{:S(2)}, u32[]{:S(2)}) collective-permute-start(f32[128,32]{0,1:T(8,128)S(1)} %get-tuple-element.247), channel_id=1, source_target_pairs={{0,8},{4,12},{8,16},{12,20},{16,24},{20,28},{24,32},{28,36},{32,40... | collective-permute-start | bytes 49160 | tf_op jit(solution)/shard_map/ppermute | solution.py:30
  231.7 8.9 %collective-permute-start.9 = (f32[128,32]{0,1:T(8,128)S(1)}, f32[128,32]{0,1:T(8,128)S(1)}, u32[]{:S(2)}, u32[]{:S(2)}) collective-permute-start(f32[128,32]{0,1:T(8,128)S(1)} %get-tuple-element.244), channel_id=1, source_target_pairs={{0,8},{4,12},{8,16},{12,20},{16,24},{20,28},{24,32},{28,36},{32,40... | collective-permute-start | bytes 49160 | tf_op jit(solution)/shard_map/ppermute | solution.py:30
Sparse Core Ops, SparseCore 0:
  9.5 83.9 all-gather.1
